TPU v7x, 512 devices: a whole 4x4x16 slice. The times are simulated.
512 devices in a mesh: ctx: 32 (over x, z_hi, core), tp: 16 (over z_lo, y).
Axes of the slice: x: 4, y: 4, z: 16 (z_hi: 4, z_lo: 4; z = z_hi * 4 + z_lo), core: 2. Of those that a mesh axis runs over, the one named last changes fastest.
Arguments:
- residual_in: bfloat16 [8192, 6144], P(('ctx', 'tp')), may hold values from -1.5 to 1.5
- query_rows: bfloat16 [8192, 4096], P('ctx', 'tp'), may hold values from -60 to 60
- key_rows: bfloat16 [8192, 4096], P('ctx', 'tp'), may hold values from -6 to 6
- value_rows: bfloat16 [8192, 4096], P('ctx', 'tp'), may hold values from -48 to 48
- out_weight: bfloat16 [4096, 6144], P('tp'), may hold values from -0.09375 to 0.09375
- gate_table: bfloat16 [64, 6144], replicated, may hold values from 0.25 to 2
- stretch_order: int32 [4], replicated, may hold values from 0 to 3, each once
- noise_levels: int32 [4], replicated, may hold values from 0 to 63
Outputs:
- mixed: bfloat16 [8192, 6144], P(('ctx', 'tp'))
Inputs may be any that keep to these rules, and one draw needn't show every extreme that they name: `stretch_order`: each place 0 to 3 once.
All inputs are finite; a program needn't handle non-finite values.
Results may differ from a plain program's by a relative error of at most 0.035.
Values may be sent and summed in bfloat16 or wider, within the bound.
A program may use at most 64 MiB of HBM per device.

v0:
```python
import math

import jax
import jax.numpy as jnp
from jax import lax
from jax.sharding import PartitionSpec as P

DH = 128


NEG = -1e30


def place_of_rows(offset, count, stretch_order, span):
    row_ids = offset + jnp.arange(count, dtype=jnp.int32)
    slots = jnp.arange(stretch_order.shape[0], dtype=jnp.int32)
    matches = (row_ids // span)[:, None] == slots[None, :]
    return jnp.sum(jnp.where(matches, stretch_order[None, :], 0), axis=1)


def partial_attention(query_block, query_place, key_block, value_block, key_place):
    count_q = query_block.shape[0]
    count_k = key_block.shape[0]
    heads = query_block.shape[1] // DH
    query_three = query_block.reshape(count_q, heads, DH)
    key_three = key_block.reshape(count_k, heads, DH)
    value_three = value_block.reshape(count_k, heads, DH)
    scores = jnp.einsum(
        "qhd,khd->qhk", query_three, key_three, preferred_element_type=jnp.float32
    ) * (1.0 / math.sqrt(DH))
    visible = (key_place[None, :] <= query_place[:, None])[:, None, :]
    scores = jnp.where(visible, scores, NEG)
    peak = jnp.max(scores, axis=2)
    weights = jnp.where(visible, jnp.exp(scores - peak[:, :, None]), 0.0)
    total = jnp.sum(weights, axis=2)
    summed = jnp.einsum(
        "qhk,khd->qhd",
        weights.astype(jnp.bfloat16),
        value_three,
        preferred_element_type=jnp.float32,
    )
    return (summed, peak, total)


def guarded_attention(query_block, query_place, key_block, value_block, key_place):
    return partial_attention(query_block, query_place, key_block, value_block, key_place)


def merge_states(older, newer):
    peak = jnp.maximum(older[1], newer[1])
    older_scale = jnp.exp(older[1] - peak)
    newer_scale = jnp.exp(newer[1] - peak)
    summed = older[0] * older_scale[:, :, None] + newer[0] * newer_scale[:, :, None]
    return (summed, peak, older[2] * older_scale + newer[2] * newer_scale)


def on_device(
    residual_in,
    query_rows,
    key_rows,
    value_rows,
    out_weight,
    gate_table,
    stretch_order,
    noise_levels,
):
    stretches = stretch_order.shape[0]
    qrows, width = query_rows.shape
    heads = width // DH
    ctx_count = lax.axis_size("ctx")
    groups = ctx_count // stretches
    span = qrows * groups
    slots = jnp.arange(stretches, dtype=jnp.int32)
    own_block = lax.axis_index("ctx") // groups
    own_place = jnp.sum(jnp.where(slots == own_block, stretch_order, 0))
    query_place = jnp.full((qrows,), own_place, jnp.int32)
    initial = (
        jnp.zeros((qrows, heads, DH), jnp.float32),
        jnp.full((qrows, heads), NEG, jnp.float32),
        jnp.zeros((qrows, heads), jnp.float32),
    )
    key_piece = lax.all_gather(key_rows, "ctx", axis=0, tiled=True)
    value_piece = lax.all_gather(value_rows, "ctx", axis=0, tiled=True)
    count = key_piece.shape[0]
    blocksize = math.gcd(count, 512)

    def advance(number, inner):
        begin = number * blocksize
        key_block = lax.dynamic_slice_in_dim(key_piece, begin, blocksize, 0)
        value_block = lax.dynamic_slice_in_dim(value_piece, begin, blocksize, 0)
        key_place = place_of_rows(begin, blocksize, stretch_order, span)
        return merge_states(
            inner, guarded_attention(query_rows, query_place, key_block, value_block, key_place)
        )

    summed, peak, total = lax.fori_loop(0, count // blocksize, advance, initial)
    attended = (summed / total[:, :, None]).reshape(qrows, width).astype(jnp.bfloat16)
    projected = lax.psum_scatter(
        jnp.dot(attended, out_weight, preferred_element_type=jnp.float32).astype(jnp.bfloat16),
        "tp",
        scatter_dimension=0,
        tiled=True,
    ).astype(jnp.float32)
    level = jnp.sum(jnp.where(slots == own_place, noise_levels, 0))
    picker = (jnp.arange(gate_table.shape[0], dtype=jnp.int32) == level).astype(jnp.bfloat16)[
        None, :
    ]
    gate = jnp.dot(picker, gate_table, preferred_element_type=jnp.float32)
    return (residual_in.astype(jnp.float32) + gate * projected).astype(jnp.bfloat16)


def solution(mesh):
    placed = (
        P(("ctx", "tp"), None),
        P("ctx", "tp"),
        P("ctx", "tp"),
        P("ctx", "tp"),
        P("tp", None),
        P(),
        P(),
        P(),
    )
    return jax.shard_map(
        on_device, mesh=mesh, in_specs=placed, out_specs=P(("ctx", "tp"), None), check_vma=False
    )
```

profile of v0, /device:TPU:6, one launch (start us, length us, event | category | flops | bytes accessed | tf_op | source)
XLA Modules:
  0.0 440.7 jit_solution(2785012970669401873)
XLA Ops:
  6.5 1.8 copy.20
  8.4 1.7 copy.21
  10.2 1.4 fusion.23
  11.6 107.4 %all-gather.3.cloned.1.call-done = bf16[8192,256]{0,1:T(8,128)(2,1)} async-done(((bf16[256,256]{0,1:T(8,128)(2,1)}), bf16[8192,256]{0,1:T(8,128)(2,1)}) %all-gather.3.cloned.1.call-update) | async-done | bytes 4194320 | tf_op jit(solution)/shard_map/all_gather | solution.py:82
  119.0 101.0 %all-gather.5.cloned.1.call-done = bf16[8192,256]{0,1:T(8,128)(2,1)} async-done(((bf16[256,256]{0,1:T(8,128)(2,1)}), bf16[8192,256]{0,1:T(8,128)(2,1)}) %all-gather.5.cloned.1.call-update) | async-done | bytes 4194320 | tf_op jit(solution)/shard_map/all_gather | solution.py:83
  219.9 118.5 %while.20 = (s32[]{:T(128)}, f32[256,2,128]{0,2,1:T(8,128)}, f32[256,2]{0,1:T(2,128)S(1)}, f32[256,2]{0,1:T(2,128)S(1)}, s32[4]{0:T(128)}, /*index=5*/bf16[8192,...) while((s32[]{:T(128)}, f32[256,2,128]{0,2,1:T(8,128)}, ...), condition=%wide.region_6.7_spmd.clone, body=%wide.region_2.6_spmd.clone.sunk | while | flops 136856576 | bytes 9607406 | solution.py:96
  219.9 1.1 constant_dynamic-slice_fusion.3
  222.5 1.3 fusion.47
  225.0 2.3 fusion.50
  227.3 1.1 constant_dynamic-slice_fusion.3
  229.8 1.3 fusion.47
  232.4 2.3 fusion.50
  234.7 1.1 constant_dynamic-slice_fusion.3
  237.2 1.3 fusion.47
  238.5 1.1 copy-done.1
  239.8 2.3 fusion.50
  242.1 1.1 constant_dynamic-slice_fusion.3
  244.6 1.3 fusion.47
  247.2 2.3 fusion.50
  249.5 1.1 constant_dynamic-slice_fusion.3
  252.1 1.3 fusion.47
  254.6 2.3 fusion.50
  256.9 1.1 constant_dynamic-slice_fusion.3
  259.5 1.3 fusion.47
  260.7 1.1 copy-done.1
  262.0 2.3 fusion.50
  264.4 1.1 constant_dynamic-slice_fusion.3
  266.9 1.3 fusion.47
  268.2 1.1 copy-done.1
  269.5 2.3 fusion.50
  271.8 1.1 constant_dynamic-slice_fusion.3
  274.3 1.3 fusion.47
  275.6 1.1 copy-done.1
  276.9 2.3 fusion.50
  279.2 1.1 constant_dynamic-slice_fusion.3
  281.7 1.3 fusion.47
  283.0 1.1 copy-done.1
  284.3 2.3 fusion.50
  286.6 1.1 constant_dynamic-slice_fusion.3
  289.1 1.3 fusion.47
  291.7 2.3 fusion.50
  294.0 1.1 constant_dynamic-slice_fusion.3
  296.5 1.3 fusion.47
  299.1 2.3 fusion.50
  301.4 1.1 constant_dynamic-slice_fusion.3
  303.9 1.3 fusion.47
  306.5 2.3 fusion.50
  308.8 1.1 constant_dynamic-slice_fusion.3
  311.3 1.3 fusion.47
  313.9 2.3 fusion.50
  316.2 1.1 constant_dynamic-slice_fusion.3
  318.8 1.3 fusion.47
  321.3 2.3 fusion.50
  323.6 1.1 constant_dynamic-slice_fusion.3
  326.2 1.3 fusion.47
  328.7 2.3 fusion.50
  331.1 1.1 constant_dynamic-slice_fusion.3
  333.6 1.3 fusion.47
  336.2 2.3 fusion.50
  339.4 2.7 convolution_convert_fusion
  342.8 1.3 fusion.24
  344.1 2.0 fusion.20
  346.1 86.4 %reduce-scatter.2.cloned.1.call-done = bf16[16,6144]{1,0:T(8,128)(2,1)} async-done(((bf16[256,6144]{1,0:T(8,128)(2,1)}), bf16[16,6144]{1,0:T(8,128)(2,1)}) %reduce-scatter.2.cloned.1.call-update) | async-done | bytes 196624 | tf_op jit(solution)/shard_map/reduce_scatter | solution.py:98
  432.5 1.7 add_convert_fusion
  (123 shorter events, 40.2 us)
Async XLA Ops:
  6.5 332.9 %copy-start = (bf16[256,6144]{1,0:T(8,128)(2,1)S(1)}, bf16[256,6144]{1,0:T(8,128)(2,1)}, u32[]{:S(2)}) copy-start(bf16[256,6144]{1,0:T(8,128)(2,1)} %param.14) | copy-start | bytes 9437188
  6.5 112.4 %all-gather.3.cloned.1.call-start = ((), (), s32[]{:S(2)}) async-start(), calls=%async_computation.1 | async-start | bytes 4325376 | tf_op jit(solution)/shard_map/all_gather | solution.py:82
  8.4 211.6 %all-gather.5.cloned.1.call-start = ((), (), s32[]{:S(2)}) async-start(), calls=%async_computation.2 | async-start | bytes 4325376 | tf_op jit(solution)/shard_map/all_gather | solution.py:83
  10.1 422.4 %reduce-scatter.2.cloned.1.call-start = ((), (), s32[]{:S(2)}) async-start(), calls=%async_computation.3 | async-start | bytes 3342336 | tf_op jit(solution)/shard_map/reduce_scatter | solution.py:98
  223.7 1.1 copy-start.1
  231.1 1.1 copy-start.1
  238.5 1.1 copy-start.1
  245.9 1.1 copy-start.1
  253.3 1.1 copy-start.1
  260.7 1.1 copy-start.1
  268.2 1.1 copy-start.1
  275.6 1.1 copy-start.1
  283.0 1.1 copy-start.1
  290.4 1.1 copy-start.1
  297.8 1.1 copy-start.1
  305.2 1.1 copy-start.1
  312.6 1.1 copy-start.1
  320.0 1.1 copy-start.1
  327.4 1.1 copy-start.1
  334.8 1.1 copy-start.1
  342.1 0.7 copy-start.3
  342.1 90.4 %copy-start.2 = (bf16[16,6144]{1,0:T(8,128)(2,1)S(1)}, bf16[16,6144]{1,0:T(8,128)(2,1)}, u32[]{:S(2)}) copy-start(bf16[16,6144]{1,0:T(8,128)(2,1)} %param.10) | copy-start | bytes 589828
Sparse Core Ops, SparseCore 0:
  10.4 108.4 all-gather.2
  122.0 97.8 all-gather.4
  342.3 90.2 reduce-scatter.1
where the time goes:
time: 442 us; the launch traced here: 441 us
  waiting for transfers between devices  295 us (67%)
  matrix products  61.8 us (14%)
  local copies, waits for them, and re-layouts  38.1 us (9%)
  other arithmetic  32.1 us (7%)
  between operations  13.2 us (3%)
    all_gather x1, waiting for transfers between devices, on_device(): key_piece = lax.all_gather(key_rows, 'ctx', axis=0, tiled=True)  107 us
    all_gather x1, waiting for transfers between devices, on_device(): value_piece = lax.all_gather(value_rows, 'ctx', axis=0, tiled=True)  101 us
    reduce_scatter x1, waiting for transfers between devices, on_device(): lax.psum_scatter(jnp.dot(attended, out_weight, preferred_element_type=jnp...  86.4 us
    dot_general x16, matrix products, partial_attention(): jnp.einsum('qhk,khd->qhd', weights.astype(jnp.bfloat16), value_three, pre...  36.9 us
    dot_general x16, matrix products, partial_attention(): jnp.einsum('qhd,khd->qhk', query_three, key_three, preferred_element_type...  20.3 us
    dynamic_slice x16, local copies, waits for them, and re-layouts, advance(): value_block = lax.dynamic_slice_in_dim(value_piece, begin, blocksize, 0)  17 us
    while x32, local copies, waits for them, and re-layouts  17 us
    reduce_sum x16, other arithmetic, place_of_rows(): return jnp.sum(jnp.where(matches, stretch_order[None, :], 0), axis=1)  11.9 us
  transfers between devices with their start and end apart: 3, of which 3 were waited for; matrix products, arithmetic and copies ran while one was open for 1% of the time, Pallas kernels for 0%

commit v1 on v0

v1 whole, which is shorter than its diff:
```python
import math

import jax
import jax.numpy as jnp
from jax import lax
from jax.experimental import pallas as pl
from jax.experimental.pallas import tpu as pltpu
from jax.sharding import PartitionSpec as P

MESH = pl.DeviceIdType.MESH
DH = 128
NEG = -1e30
SCALE = math.log2(math.e) / math.sqrt(DH)
F32 = jnp.float32
BF16 = jnp.bfloat16


def remote(src, dst, sems, device):
    return pltpu.make_async_remote_copy(
        src_ref=src,
        dst_ref=dst,
        send_sem=sems[0],
        recv_sem=sems[1],
        device_id=device,
        device_id_type=MESH,
    )


def kernel(
    res_in,
    q_in,
    k_in,
    v_in,
    w_in,
    gate_in,
    order_ref,
    noise_ref,
    out_ref,
    qbuf,
    kbuf,
    vbuf,
    acc,
    lsum,
    peak,
    osend,
    lsend,
    oret,
    lret,
    abuf,
    wbuf,
    pbuf,
    rbuf,
    gbuf,
    gsel,
    resbuf,
    local_sem,
    sib_sem,
    par_sem,
    crs_sem,
    qx_sem,
    ox_sem,
    lx_sem,
    z_sem,
    a_sem,
    w_sem,
    wf_sem,
    r_sem,
):
    ctx = lax.axis_index("ctx")
    tp = lax.axis_index("tp")
    x = ctx // 8
    zh = (ctx // 2) % 4
    core = ctx % 2
    zl = tp // 4
    y = tp % 4
    head = zh // 2
    mine = pl.ds(pl.multiple_of(head * DH, DH), DH)
    other = pl.ds(pl.multiple_of((1 - head) * DH, DH), DH)
    sib = (ctx + 1 - 2 * core, tp)
    par = (ctx + 2 - 4 * (zh % 2), tp)
    crs = (ctx + 6 - 4 * zh, tp)
    rows = q_in.shape[0]
    half = rows // 2
    slab = wbuf.shape[1]

    def xpeer(dx):
        return (((x + dx) % 4) * 8 + zh * 2 + core, tp)

    def ypeer(dy):
        return (ctx, zl * 4 + (y + dy) % 4)

    def tpeer(dz, dy):
        return (ctx, ((zl + dz) % 4) * 4 + (y + dy) % 4)

    def columns(index):
        return pl.ds(pl.multiple_of(index * slab, slab), slab)

    locals_ = [
        pltpu.make_async_copy(q_in.at[:, mine], qbuf.at[0], local_sem.at[0]),
        pltpu.make_async_copy(k_in.at[:, mine], kbuf.at[0, 0], local_sem.at[1]),
        pltpu.make_async_copy(v_in.at[:, mine], vbuf.at[0, 0], local_sem.at[2]),
        pltpu.make_async_copy(w_in.at[:, columns(y)], wbuf.at[pl.ds(0, rows)], local_sem.at[3]),
        pltpu.make_async_copy(gate_in, gbuf, local_sem.at[4]),
        pltpu.make_async_copy(res_in, resbuf, local_sem.at[5]),
    ]
    for copy in locals_:
        copy.start()

    barrier = pltpu.get_barrier_semaphore()
    partners = [sib, par, crs] + [xpeer(dx) for dx in (1, 2, 3)]
    for partner in partners:
        pl.semaphore_signal(barrier, inc=1, device_id=partner, device_id_type=MESH)

    def greet(step, carry):
        pl.semaphore_signal(
            barrier, inc=1, device_id=tpeer(step // 4, step % 4), device_id_type=MESH
        )
        return carry

    lax.fori_loop(1, 16, greet, 0)
    pl.semaphore_wait(barrier, len(partners) + 15)

    q_cross = remote(q_in.at[:, other], qbuf.at[4], (crs_sem.at[0, 0], crs_sem.at[1, 0]), crs)
    k_cross = remote(k_in.at[:, other], kbuf.at[2, 0], (crs_sem.at[0, 1], crs_sem.at[1, 1]), crs)
    v_cross = remote(v_in.at[:, other], vbuf.at[2, 0], (crs_sem.at[0, 2], crs_sem.at[1, 2]), crs)
    k_pair = remote(k_in.at[:, mine], kbuf.at[1, 0], (par_sem.at[0, 0], par_sem.at[1, 0]), par)
    v_pair = remote(v_in.at[:, mine], vbuf.at[1, 0], (par_sem.at[0, 1], par_sem.at[1, 1]), par)
    k_far = remote(kbuf.at[2, 0], kbuf.at[3, 0], (par_sem.at[0, 2], par_sem.at[1, 2]), par)
    v_far = remote(vbuf.at[2, 0], vbuf.at[3, 0], (par_sem.at[0, 3], par_sem.at[1, 3]), par)

    def share(buf, role, number):
        src = buf.at[role, 0]
        if role == 0:
            src = (k_in if number == 0 else v_in).at[:, mine]
        index = 2 * role + number
        return remote(src, buf.at[role, 1], (sib_sem.at[0, index], sib_sem.at[1, index]), sib)

    k_share = [share(kbuf, role, 0) for role in range(4)]
    v_share = [share(vbuf, role, 1) for role in range(4)]

    def q_across(part, dx):
        index = part * 3 + dx - 1
        src = q_in.at[:, mine] if part == 0 else qbuf.at[4]
        return remote(
            src, qbuf.at[4 * part + dx], (qx_sem.at[0, index], qx_sem.at[1, index]), xpeer(dx)
        )

    def w_send(dy):
        own_half = pl.ds(pl.multiple_of(half * core, half), half)
        there = pl.ds(pl.multiple_of(dy * rows + half * core, half), half)
        return remote(
            w_in.at[own_half, columns((y + dy) % 4)],
            wbuf.at[there],
            (w_sem.at[0, dy - 1], w_sem.at[1, dy - 1]),
            ypeer(dy),
        )

    def w_share(dy):
        there = pl.ds(pl.multiple_of(dy * rows + half * core, half), half)
        return remote(wbuf.at[there], wbuf.at[there], (wf_sem.at[0, dy - 1], wf_sem.at[1, dy - 1]), sib)

    q_cross.start()
    k_pair.start()
    k_cross.start()
    v_pair.start()
    v_cross.start()
    k_share[0].start()
    v_share[0].start()
    for dx in (1, 2, 3):
        q_across(0, dx).start()
    for dy in (1, 2, 3):
        w_send(dy).start()

    def block(b, role):
        k = kbuf[role].reshape(2 * rows, DH)
        v = vbuf[role].reshape(2 * rows, DH)
        count = 2 * rows // DH
        for top in range(0, rows, half):
            at = pl.ds(top, half)
            s = (
                lax.dot_general(
                    qbuf[b, at], k, (((1,), (1,)), ((), ())), preferred_element_type=F32
                )
                * SCALE
            )
            top_now = jnp.max(s, axis=1, keepdims=True)
            if role == 0:
                m = jnp.broadcast_to(top_now, (half, DH))
            else:
                m = jnp.maximum(peak[b, at], top_now)
                fade = jnp.exp2(peak[b, at] - m)
            p = jnp.exp2(s - jnp.concatenate([m] * count, axis=1))
            total = p[:, :DH]
            for part in range(1, count):
                total = total + p[:, part * DH : (part + 1) * DH]
            summed = jnp.dot(p.astype(BF16), v, preferred_element_type=F32)
            if role > 0:
                total = total + lsum[b, at] * fade
                summed = summed + acc[b, at] * fade
            if role < 3:
                peak[b, at] = m
                lsum[b, at] = total
                acc[b, at] = summed
            else:
                total = jnp.broadcast_to(jnp.sum(total, axis=1, keepdims=True), (half, DH))
                osend[b, at] = (summed / total).astype(BF16)
                lse = m + jnp.log2(total)
                lsend[b, pl.ds(top // half, 1)] = lse.T[:1]

    def blocks(first, count, role):
        def step(i, carry):
            block(first + i, role)
            return carry

        lax.fori_loop(0, count, step, 0)

    locals_[0].wait()
    locals_[1].wait()
    locals_[2].wait()
    k_share[0].wait_recv()
    v_share[0].wait_recv()
    for dx in (1, 2, 3):
        q_across(0, dx).wait_recv()
    blocks(0, 4, 0)

    q_cross.wait_recv()
    for dx in (1, 2, 3):
        q_across(1, dx).start()

    locals_[4].wait()
    place = order_ref[x]
    level = noise_ref[0] * 0
    for slot in range(4):
        level = level + jnp.where(place == slot, noise_ref[slot], 0)
    levels = gbuf.shape[0]
    picker = (lax.broadcasted_iota(jnp.int32, (16, levels), 1) == level).astype(BF16)
    for piece in range(4):
        at = pl.ds(piece * slab, slab)
        gsel[:, at] = jnp.dot(picker, gbuf[:, at], preferred_element_type=F32)

    k_pair.wait_recv()
    k_share[1].start()
    v_pair.wait_recv()
    v_share[1].start()
    k_cross.wait_recv()
    k_far.start()
    k_share[2].start()
    for dx in (1, 2, 3):
        q_across(1, dx).wait_recv()
    blocks(4, 4, 0)
    k_share[1].wait_recv()
    v_share[1].wait_recv()
    blocks(0, 4, 1)
    v_cross.wait_recv()
    v_far.start()
    v_share[2].start()
    blocks(4, 4, 1)
    k_share[2].wait_recv()
    v_share[2].wait_recv()
    blocks(0, 8, 2)
    for dy in (1, 2, 3):
        w_send(dy).wait_recv()
        w_share(dy).start()
    k_far.wait_recv()
    k_share[3].start()
    v_far.wait_recv()
    v_share[3].start()
    k_share[3].wait_recv()
    v_share[3].wait_recv()

    def o_back(part, dx):
        index = part * 3 + dx - 1
        b = 4 * part + dx
        return remote(
            osend.at[b], oret.at[index], (ox_sem.at[0, index], ox_sem.at[1, index]), xpeer(4 - dx)
        )

    def l_back(part, dx):
        index = part * 3 + dx - 1
        b = 4 * part + dx
        return remote(
            lsend.at[b], lret.at[index], (lx_sem.at[0, index], lx_sem.at[1, index]), xpeer(4 - dx)
        )

    for part in (1, 0):

        def last(i, carry):
            block(4 * part + 1 + i, 3)
            l_back(part, 1 + i).start()
            o_back(part, 1 + i).start()
            return carry

        lax.fori_loop(0, 3, last, 0)
        block(4 * part, 3)

    def merged(part, top):
        at = pl.ds(top, half)
        line = pl.ds(top // half, 1)
        states = [(lsend[4 * part, line], osend[4 * part, at])]
        for dx in (1, 2, 3):
            index = part * 3 + dx - 1
            seen = order_ref[(x + dx) % 4] <= place
            states.append((jnp.where(seen, lret[index, line], NEG), oret[index, at]))
        top_lse = states[0][0]
        for lse, _ in states[1:]:
            top_lse = jnp.maximum(top_lse, lse)
        total = jnp.zeros((half, DH), F32)
        result = jnp.zeros((half, DH), F32)
        for lse, value in states:
            share_of = jnp.broadcast_to(jnp.exp2(lse - top_lse), (DH, DH)).T
            total = total + share_of
            result = result + share_of * value.astype(F32)
        return (result / total).astype(BF16)

    back = remote(
        osend.at[4], abuf.at[:, mine], (z_sem.at[0], z_sem.at[1]), crs
    )
    for dx in (1, 2, 3):
        l_back(1, dx).wait_recv()
        o_back(1, dx).wait_recv()
    for top in range(0, rows, half):
        osend[4, pl.ds(top, half)] = merged(1, top)
    back.start()

    def a_send(which, dy):
        index = which * 3 + dy - 1
        lane = head if which == 0 else 1 - head
        there = pl.ds(pl.multiple_of(dy * 2 * DH + lane * DH, DH), DH)
        return remote(
            abuf.at[:, mine if which == 0 else other],
            abuf.at[:, there],
            (a_sem.at[0, index], a_sem.at[1, index]),
            ypeer(dy),
        )

    for dx in (1, 2, 3):
        l_back(0, dx).wait_recv()
        o_back(0, dx).wait_recv()
    for top in range(0, rows, half):
        abuf[pl.ds(top, half), mine] = merged(0, top)
    for dy in (1, 2, 3):
        a_send(0, dy).start()
    back.wait_recv()
    for dy in (1, 2, 3):
        a_send(1, dy).start()

    locals_[3].wait()
    for dy in (1, 2, 3):
        w_share(dy).wait_recv()
    for dy in (1, 2, 3):
        a_send(0, dy).wait_recv()
        a_send(1, dy).wait_recv()

    piece_width = 256

    def project(i, carry):
        at = pl.ds(pl.multiple_of(i * piece_width, piece_width), piece_width)
        pbuf[:, at] = jnp.dot(abuf[...], wbuf[:, at], preferred_element_type=F32).astype(BF16)
        return carry

    lax.fori_loop(0, slab // piece_width, project, 0)

    def r_send(step):
        there = tpeer(step // 4, step % 4)
        first = pl.ds(pl.multiple_of(there[1] * 16, 16), 16)
        return remote(
            pbuf.at[first], rbuf.at[step], (r_sem.at[0, step], r_sem.at[1, step]), there
        )

    def r_start(step, carry):
        r_send(step).start()
        return carry

    lax.fori_loop(1, 16, r_start, 0)

    own_rows = pl.ds(pl.multiple_of(tp * 16, 16), 16)
    rbuf[0] = pbuf[own_rows]

    def r_wait(step, carry):
        r_send(step).wait_recv()
        return carry

    lax.fori_loop(1, 16, r_wait, 0)
    locals_[5].wait()
    for dy in range(4):
        at = columns((y + 4 - dy) % 4)
        projected = rbuf[dy].astype(F32)
        for dz in (1, 2, 3):
            projected = projected + rbuf[4 * dz + dy].astype(F32)
        mixed = resbuf[:, at].astype(F32) + gsel[:, at] * projected
        out_ref[:, at] = mixed.astype(BF16)

    for copy in [q_cross, k_cross, v_cross, k_pair, v_pair, k_far, v_far, back]:
        copy.wait_send()
    for copy in k_share + v_share:
        copy.wait_send()
    for step in (1, 2, 3):
        w_send(step).wait_send()
        w_share(step).wait_send()
        for part in (0, 1):
            q_across(part, step).wait_send()
            o_back(part, step).wait_send()
            l_back(part, step).wait_send()
            a_send(part, step).wait_send()

    def r_left(step, carry):
        r_send(step).wait_send()
        return carry

    lax.fori_loop(1, 16, r_left, 0)


def on_device(
    residual_in,
    query_rows,
    key_rows,
    value_rows,
    out_weight,
    gate_table,
    stretch_order,
    noise_levels,
):
    rows = query_rows.shape[0]
    width = residual_in.shape[1]
    slab = width // 4
    any_spec = pl.BlockSpec(memory_space=pl.ANY)
    smem_spec = pl.BlockSpec(memory_space=pltpu.SMEM)
    dma = pltpu.SemaphoreType.DMA
    return pl.pallas_call(
        kernel,
        out_shape=jax.ShapeDtypeStruct(residual_in.shape, BF16),
        in_specs=[any_spec] * 6 + [smem_spec] * 2,
        out_specs=pl.BlockSpec(memory_space=pltpu.VMEM),
        scratch_shapes=[
            pltpu.VMEM((8, rows, DH), BF16),
            pltpu.VMEM((4, 2, rows, DH), BF16),
            pltpu.VMEM((4, 2, rows, DH), BF16),
            pltpu.VMEM((8, rows, DH), F32),
            pltpu.VMEM((8, rows, DH), F32),
            pltpu.VMEM((8, rows, DH), F32),
            pltpu.VMEM((8, rows, DH), BF16),
            pltpu.VMEM((8, 8, DH), F32),
            pltpu.VMEM((6, rows, DH), BF16),
            pltpu.VMEM((6, 8, DH), F32),
            pltpu.VMEM((rows, 8 * DH), BF16),
            pltpu.VMEM((4 * rows, slab), BF16),
            pltpu.VMEM((rows, slab), BF16),
            pltpu.VMEM((16, 16, slab), BF16),
            pltpu.VMEM(gate_table.shape, BF16),
            pltpu.VMEM((16, width), F32),
            pltpu.VMEM(residual_in.shape, BF16),
            dma((6,)),
            dma((2, 8)),
            dma((2, 4)),
            dma((2, 3)),
            dma((2, 6)),
            dma((2, 6)),
            dma((2, 6)),
            dma((2,)),
            dma((2, 6)),
            dma((2, 3)),
            dma((2, 3)),
            dma((2, 16)),
        ],
        compiler_params=pltpu.CompilerParams(
            collective_id=0, has_side_effects=True, vmem_limit_bytes=48 * 1024 * 1024
        ),
        name="sublayer",
    )(
        residual_in,
        query_rows,
        key_rows,
        value_rows,
        out_weight,
        gate_table,
        stretch_order,
        noise_levels,
    )


def solution(mesh):
    placed = (
        P(("ctx", "tp"), None),
        P("ctx", "tp"),
        P("ctx", "tp"),
        P("ctx", "tp"),
        P("tp", None),
        P(),
        P(),
        P(),
    )
    return jax.shard_map(
        on_device, mesh=mesh, in_specs=placed, out_specs=P(("ctx", "tp"), None), check_vma=False
    )
```

time: 442 us -> 98.7 us (0.22)
  the two profiles are of different devices: /device:TPU:6 before, /device:TPU:66 now
where the time goes in v1:
time: 98.7 us; the launch traced here: 98.4 us
  Pallas kernels  89.8 us (91%)
  local copies, waits for them, and re-layouts  8.65 us (9%)
    pallas_call x1, Pallas kernels, on_device(): pl.pallas_call(kernel, out_shape=jax.ShapeDtypeStruct(residual_in.shape,...  89.8 us
    unnamed x17, local copies, waits for them, and re-layouts  8.65 us

profile of v1, /device:TPU:66, one launch (start us, length us, event | category | flops | bytes accessed | tf_op | source)
XLA Modules:
  0.0 98.4 jit_solution(8187861278976896989)
XLA Ops:
  0.0 0.0 copy-start
  0.0 1.9 %copy-done = bf16[256,6144]{1,0:T(8,128)(2,1)S(1)} copy-done((bf16[256,6144]{1,0:T(8,128)(2,1)S(1)}, bf16[256,6144]{1,0:T(8,128)(2,1)}, u32[]{:S(2)}) %copy-start) | copy-done | bytes 3145752
  1.9 0.0 copy-start.1
  1.9 1.1 %copy-done.1 = bf16[64,6144]{1,0:T(8,128)(2,1)S(1)} copy-done((bf16[64,6144]{1,0:T(8,128)(2,1)S(1)}, bf16[64,6144]{1,0:T(8,128)(2,1)}, u32[]{:S(2)}) %copy-start.1) | copy-done | bytes 786456
  3.0 0.0 copy-start.2
  3.0 0.9 copy-done.2
  4.0 0.0 copy-start.3
  4.0 0.9 copy-done.3
  4.9 0.0 copy-start.4
  4.9 0.9 copy-done.4
  5.8 0.0 copy-start.5
  5.8 0.9 copy-done.5
  6.7 0.0 copy-start.6
  6.7 0.7 copy-done.6
  7.3 0.0 copy-start.7
  7.3 0.7 copy-done.7
  8.0 89.8 %sublayer.1 = bf16[16,6144]{1,0:T(8,128)(2,1)S(1)} custom-call(bf16[16,6144]{1,0:T(8,128)(2,1)S(1)} %copy-done.2, bf16[256,256]{1,0:T(8,128)(2,1)S(1)} %copy-done.3, bf16[256,256]{1,0:T(8,128)(2,1)S(1)} %copy-done.4, bf16[256,256]{1,0:T(8,128)(2,1)S(1)} %copy-done.5, bf16[256,6144]{1,0:T(8,128)(2,1)S(1)} %copy-done, bf16[64,6144]{1,0:T(8,128)(2,1)S(1)} %copy-done.1, ...), custom_call_target="tpu_custom_call" | custom-call | tf_op jit(solution)/shard_map/sublayer/pallas_call | solution.py:429
  97.8 0.7 copy.10
Async XLA Ops:
  0.0 1.9 %copy-start = (bf16[256,6144]{1,0:T(8,128)(2,1)S(1)}, bf16[256,6144]{1,0:T(8,128)(2,1)}, u32[]{:S(2)}) copy-start(bf16[256,6144]{1,0:T(8,128)(2,1)} %w_in.1) | copy-start | bytes 9437188
  1.9 1.1 %copy-start.1 = (bf16[64,6144]{1,0:T(8,128)(2,1)S(1)}, bf16[64,6144]{1,0:T(8,128)(2,1)}, u32[]{:S(2)}) copy-start(bf16[64,6144]{1,0:T(8,128)(2,1)} %gate_in.1) | copy-start | bytes 2359300
  3.0 0.9 copy-start.2
  4.0 0.9 copy-start.3
  4.9 0.9 copy-start.4
  5.8 0.9 copy-start.5
  6.7 0.7 copy-start.6
  7.3 0.7 copy-start.7

commit v2 on v1

v2 whole, which is shorter than its diff:
```python
import functools
import math

import jax
import jax.numpy as jnp
from jax import lax
from jax.experimental import pallas as pl
from jax.experimental.pallas import tpu as pltpu
from jax.sharding import PartitionSpec as P

MESH = pl.DeviceIdType.MESH
DH = 128
NEG = -1e30
SCALE = math.log2(math.e) / math.sqrt(DH)
F32 = jnp.float32
BF16 = jnp.bfloat16


def remote(src, dst, sems, device):
    return pltpu.make_async_remote_copy(
        src_ref=src,
        dst_ref=dst,
        send_sem=sems[0],
        recv_sem=sems[1],
        device_id=device,
        device_id_type=MESH,
    )


def kernel(
    res_in,
    q_in,
    k_in,
    v_in,
    w_in,
    gate_in,
    order_ref,
    noise_ref,
    out_ref,
    qbuf,
    kbuf,
    vbuf,
    acc,
    lsum,
    peak,
    osend,
    lsend,
    oret,
    lret,
    zsend,
    abuf,
    wbuf,
    pbuf,
    rbuf,
    gbuf,
    gsel,
    resbuf,
    local_sem,
    sib_sem,
    par_sem,
    crs_sem,
    qx_sem,
    ox_sem,
    lx_sem,
    z_sem,
    a_sem,
    w_sem,
    wf_sem,
    r_sem,
):
    ctx = lax.axis_index("ctx")
    tp = lax.axis_index("tp")
    x = ctx // 8
    zh = (ctx // 2) % 4
    core = ctx % 2
    zl = tp // 4
    y = tp % 4
    odd = zl % 2
    ring = (zh + odd) % 4
    head = ring // 2
    mine = pl.ds(pl.multiple_of(head * DH, DH), DH)
    other = pl.ds(pl.multiple_of((1 - head) * DH, DH), DH)

    def at_ring(place):
        return (x * 8 + ((place + 4 - odd) % 4) * 2 + core, tp)

    sib = (ctx + 1 - 2 * core, tp)
    par = at_ring(ring + 1 - 2 * (ring % 2))
    crs = at_ring(3 - ring)
    rows = k_in.shape[0]
    half = rows // 2
    slab = wbuf.shape[1]

    def xpeer(dx):
        return (((x + dx) % 4) * 8 + zh * 2 + core, tp)

    def ypeer(dy):
        return (ctx, zl * 4 + (y + dy) % 4)

    def tpeer(dz, dy):
        return (ctx, ((zl + dz) % 4) * 4 + (y + dy) % 4)

    def columns(index):
        return pl.ds(pl.multiple_of(index * slab, slab), slab)

    started = []

    def send(copy):
        copy.start()
        started.append(copy)

    def got(copy):
        copy.wait_recv()

    def here(index):
        locals_[index].wait()


    def finish():
        for copy in started:
            copy.wait_send()

    locals_ = [
        pltpu.make_async_copy(q_in.at[:, :, :, mine], qbuf.at[0, 0], local_sem.at[0]),
        pltpu.make_async_copy(k_in.at[:, mine], kbuf.at[0, 0], local_sem.at[1]),
        pltpu.make_async_copy(v_in.at[:, mine], vbuf.at[0, 0], local_sem.at[2]),
        pltpu.make_async_copy(w_in.at[:, columns(y)], wbuf.at[pl.ds(0, rows)], local_sem.at[3]),
        pltpu.make_async_copy(gate_in, gbuf, local_sem.at[4]),
        pltpu.make_async_copy(res_in, resbuf, local_sem.at[5]),
    ]
    for copy in locals_:
        copy.start()

    barrier = pltpu.get_barrier_semaphore()
    partners = [sib, par, crs] + [xpeer(dx) for dx in (1, 2, 3)]
    for partner in partners:
        pl.semaphore_signal(barrier, inc=1, device_id=partner, device_id_type=MESH)

    def greet(step, carry):
        pl.semaphore_signal(
            barrier, inc=1, device_id=tpeer(step // 4, step % 4), device_id_type=MESH
        )
        return carry

    lax.fori_loop(1, 16, greet, 0)
    pl.semaphore_wait(barrier, len(partners) + 15)

    q_cross = remote(q_in.at[:, :, :, other], qbuf.at[0, 1], (crs_sem.at[0, 0], crs_sem.at[1, 0]), crs)
    k_cross = remote(k_in.at[:, other], kbuf.at[2, 0], (crs_sem.at[0, 1], crs_sem.at[1, 1]), crs)
    v_cross = remote(v_in.at[:, other], vbuf.at[2, 0], (crs_sem.at[0, 2], crs_sem.at[1, 2]), crs)
    k_pair = remote(k_in.at[:, mine], kbuf.at[1, 0], (par_sem.at[0, 0], par_sem.at[1, 0]), par)
    v_pair = remote(v_in.at[:, mine], vbuf.at[1, 0], (par_sem.at[0, 1], par_sem.at[1, 1]), par)
    k_far = remote(kbuf.at[2, 0], kbuf.at[3, 0], (par_sem.at[0, 2], par_sem.at[1, 2]), par)
    v_far = remote(vbuf.at[2, 0], vbuf.at[3, 0], (par_sem.at[0, 3], par_sem.at[1, 3]), par)

    def share(buf, role, number):
        src = buf.at[role, 0]
        if role == 0:
            src = (k_in if number == 0 else v_in).at[:, mine]
        index = 2 * role + number
        return remote(src, buf.at[role, 1], (sib_sem.at[0, index], sib_sem.at[1, index]), sib)

    k_share = [share(kbuf, role, 0) for role in range(4)]
    v_share = [share(vbuf, role, 1) for role in range(4)]

    @functools.cache
    def q_across(part, dx):
        index = part * 3 + dx - 1
        src = q_in.at[:, :, :, mine] if part == 0 else qbuf.at[0, 1]
        return remote(
            src, qbuf.at[dx, part], (qx_sem.at[0, index], qx_sem.at[1, index]), xpeer(dx)
        )

    @functools.cache
    def w_send(dy):
        own_half = pl.ds(pl.multiple_of(half * core, half), half)
        there = pl.ds(pl.multiple_of(dy * rows + half * core, half), half)
        return remote(
            w_in.at[own_half, columns((y + dy) % 4)],
            wbuf.at[there],
            (w_sem.at[0, dy - 1], w_sem.at[1, dy - 1]),
            ypeer(dy),
        )

    @functools.cache
    def w_share(dy):
        there = pl.ds(pl.multiple_of(dy * rows + half * core, half), half)
        return remote(wbuf.at[there], wbuf.at[there], (wf_sem.at[0, dy - 1], wf_sem.at[1, dy - 1]), sib)

    send(k_pair)
    send(k_cross)
    send(v_pair)
    send(v_cross)
    send(q_cross)
    send(k_share[0])
    send(v_share[0])
    for dx in (1, 2, 3):
        send(q_across(0, dx))
    for dy in (1, 2, 3):
        send(w_send(dy))

    batch = 4 * rows

    def attend(role, spot):

        def load(ref):
            return ref[spot].reshape(batch, DH)

        k = kbuf[role].reshape(2 * rows, DH)
        v = vbuf[role].reshape(2 * rows, DH)
        count = 2 * rows // DH
        s = (
            lax.dot_general(load(qbuf), k, (((1,), (1,)), ((), ())), preferred_element_type=F32)
            * SCALE
        )
        m = jnp.broadcast_to(jnp.max(s, axis=1, keepdims=True), (batch, DH))
        if role > 0:
            before = load(peak)
            m = jnp.maximum(before, m)
            fade = jnp.exp2(before - m)
        p = jnp.exp2(s - jnp.concatenate([m] * count, axis=1))
        total = p[:, :DH]
        for part in range(1, count):
            total = total + p[:, part * DH : (part + 1) * DH]
        summed = jnp.dot(p.astype(BF16), v, preferred_element_type=F32)
        if role > 0:
            total = total + load(lsum) * fade
            summed = summed + load(acc) * fade
        return m, total, summed

    def attend_part(role, part):
        spot = (slice(None), part)
        m, total, summed = attend(role, spot)
        for ref, value in ((peak, m), (lsum, total), (acc, summed)):
            ref[spot] = value.reshape(ref[spot].shape)

    here(0)
    here(1)
    here(2)
    got(k_share[0])
    got(v_share[0])
    for dx in (1, 2, 3):
        got(q_across(0, dx))
    attend_part(0, 0)

    got(k_cross)
    send(k_far)
    send(k_share[2])
    got(k_pair)
    send(k_share[1])
    got(v_cross)
    send(v_far)
    send(v_share[2])
    got(v_pair)
    send(v_share[1])
    here(4)
    place = order_ref[x]
    level = noise_ref[0] * 0
    for slot in range(4):
        level = level + jnp.where(place == slot, noise_ref[slot], 0)
    levels = gbuf.shape[0]
    picker = (lax.broadcasted_iota(jnp.int32, (16, levels), 1) == level).astype(BF16)
    for piece in range(4):
        at = pl.ds(piece * slab, slab)
        gsel[:, at] = jnp.dot(picker, gbuf[:, at], preferred_element_type=F32)

    got(q_cross)
    for dx in (1, 2, 3):
        send(q_across(1, dx))
    got(k_share[1])
    got(v_share[1])
    attend_part(1, 0)
    got(k_share[2])
    got(v_share[2])
    attend_part(2, 0)
    for dx in (1, 2, 3):
        got(q_across(1, dx))
    attend_part(0, 1)
    got(k_far)
    send(k_share[3])
    attend_part(1, 1)
    got(v_far)
    send(v_share[3])
    attend_part(2, 1)
    got(k_share[3])
    got(v_share[3])

    @functools.cache
    def o_back(j, dx):
        index = j * 3 + dx - 1
        return remote(
            osend.at[j, dx],
            oret.at[j, dx - 1],
            (ox_sem.at[0, index], ox_sem.at[1, index]),
            xpeer(4 - dx),
        )

    @functools.cache
    def l_back(j, dx):
        index = j * 3 + dx - 1
        return remote(
            lsend.at[j, dx],
            lret.at[j, dx - 1],
            (lx_sem.at[0, index], lx_sem.at[1, index]),
            xpeer(4 - dx),
        )

    for j in (0, 1):
        m, total, summed = attend(3, (slice(None), slice(None), slice(None), j))
        total = jnp.sum(total, axis=1, keepdims=True)
        osend[j] = (summed * (1.0 / total)).astype(BF16).reshape(4, 2, half, DH)
        lse = m + jnp.log2(total)
        for dx in range(4):
            for part in (0, 1):
                first = (2 * dx + part) * half
                lsend[j, dx, part : part + 1] = lse[first : first + half].T[:1]
        for dx in (1, 2, 3):
            send(l_back(j, dx))
            send(o_back(j, dx))
        if j == 0:
            for dy in (1, 2, 3):
                got(w_send(dy))
                send(w_share(dy))


    seen = [order_ref[(x + dx) % 4] <= place for dx in (1, 2, 3)]

    def merged(j, part):
        states = [(lsend[j, 0, part : part + 1], osend[j, 0, part])]
        for dx in (1, 2, 3):
            lse = jnp.where(seen[dx - 1], lret[j, dx - 1, part : part + 1], NEG)
            states.append((lse, oret[j, dx - 1, part]))
        highest = states[0][0]
        for lse, _ in states[1:]:
            highest = jnp.maximum(highest, lse)
        shares = [jnp.exp2(lse - highest) for lse, _ in states]
        total = shares[0] + shares[1] + shares[2] + shares[3]
        result = jnp.zeros((half, DH), F32)
        for weight, (_, value) in zip(shares, states):
            result = result + jnp.broadcast_to(weight / total, (DH, DH)).T * value.astype(F32)
        return result.astype(BF16)

    def back(j):
        return remote(zsend.at[j], abuf.at[j, :, mine], (z_sem.at[0, j], z_sem.at[1, j]), crs)

    @functools.cache
    def a_send(j, which, dy):
        index = (2 * j + which) * 3 + dy - 1
        lane = head if which == 0 else 1 - head
        there = pl.ds(pl.multiple_of(dy * 2 * DH + lane * DH, DH), DH)
        return remote(
            abuf.at[j, :, mine if which == 0 else other],
            abuf.at[j, :, there],
            (a_sem.at[0, index], a_sem.at[1, index]),
            ypeer(dy),
        )

    backs = [back(0), back(1)]
    for j in (0, 1):
        for dx in (1, 2, 3):
            got(l_back(j, dx))
            got(o_back(j, dx))
        zsend[j] = merged(j, 1)
        send(backs[j])
        abuf[j, :, mine] = merged(j, 0)
        for dy in (1, 2, 3):
            send(a_send(j, 0, dy))
    for j in (0, 1):
        got(backs[j])
        for dy in (1, 2, 3):
            send(a_send(j, 1, dy))

    here(3)
    for dy in (1, 2, 3):
        got(w_share(dy))


    piece_width = 512

    def r_send(step):
        there = tpeer(step // 4, step % 4)
        to_y = there[1] % 4
        first = pl.ds(pl.multiple_of((there[1] // 4) * 32 + (to_y % 2) * 16, 16), 16)
        return remote(
            pbuf.at[to_y // 2, first],
            rbuf.at[step],
            (r_sem.at[0, step], r_sem.at[1, step]),
            there,
        )

    for j in (0, 1):
        for dy in (1, 2, 3):
            got(a_send(j, 0, dy))
            got(a_send(j, 1, dy))

        def project(i, carry):
            at = pl.ds(pl.multiple_of(i * piece_width, piece_width), piece_width)
            pbuf[j, :, at] = jnp.dot(abuf[j], wbuf[:, at], preferred_element_type=F32).astype(BF16)
            return carry

        lax.fori_loop(0, slab // piece_width, project, 0)

        def r_start(i, carry):
            dz = (i // 2 + 1) % 4
            step = dz * 4 + (2 * j + i % 2 + 4 - y) % 4

            @pl.when(step != 0)
            def _():
                r_send(step).start()

            return carry

        lax.fori_loop(0, 8, r_start, 0)

    own_rows = pl.ds(pl.multiple_of(zl * 32 + (y % 2) * 16, 16), 16)
    rbuf[0] = pbuf[y // 2, own_rows]

    here(5)
    for dy in (3, 2, 1, 0):
        at = columns((y + 4 - dy) % 4)
        for dz in range(4):
            if dz + dy > 0:
                r_send(4 * dz + dy).wait_recv()
        projected = rbuf[dy].astype(F32)
        for dz in (1, 2, 3):
            projected = projected + rbuf[4 * dz + dy].astype(F32)
        mixed = resbuf[:, at].astype(F32) + gsel[:, at] * projected
        out_ref[:, at] = mixed.astype(BF16)

    finish()

    def r_left(step, carry):
        r_send(step).wait_send()
        return carry

    lax.fori_loop(1, 16, r_left, 0)


def on_device(
    residual_in,
    query_rows,
    key_rows,
    value_rows,
    out_weight,
    gate_table,
    stretch_order,
    noise_levels,
):
    rows, width_in = query_rows.shape
    width = residual_in.shape[1]
    slab = width // 4
    any_spec = pl.BlockSpec(memory_space=pltpu.HBM)
    smem_spec = pl.BlockSpec(memory_space=pltpu.SMEM)
    dma = pltpu.SemaphoreType.DMA
    return pl.pallas_call(
        kernel,
        out_shape=jax.ShapeDtypeStruct(residual_in.shape, BF16),
        in_specs=[any_spec] * 6 + [smem_spec] * 2,
        out_specs=pl.BlockSpec(memory_space=pltpu.VMEM),
        scratch_shapes=[
            pltpu.VMEM((4, 2, 4, 2, rows // 8, DH), BF16),
            pltpu.VMEM((4, 2, rows, DH), BF16),
            pltpu.VMEM((4, 2, rows, DH), BF16),
            pltpu.VMEM((4, 2, 4, 2, rows // 8, DH), F32),
            pltpu.VMEM((4, 2, 4, 2, rows // 8, DH), F32),
            pltpu.VMEM((4, 2, 4, 2, rows // 8, DH), F32),
            pltpu.VMEM((2, 4, 2, rows // 2, DH), BF16),
            pltpu.VMEM((2, 4, 8, DH), F32),
            pltpu.VMEM((2, 3, 2, rows // 2, DH), BF16),
            pltpu.VMEM((2, 3, 8, DH), F32),
            pltpu.VMEM((2, rows // 2, DH), BF16),
            pltpu.VMEM((2, rows // 2, 8 * DH), BF16),
            pltpu.VMEM((4 * rows, slab), BF16),
            pltpu.VMEM((2, rows // 2, slab), BF16),
            pltpu.VMEM((16, 16, slab), BF16),
            pltpu.VMEM(gate_table.shape, BF16),
            pltpu.VMEM((16, width), F32),
            pltpu.VMEM(residual_in.shape, BF16),
            dma((6,)),
            dma((2, 8)),
            dma((2, 4)),
            dma((2, 3)),
            dma((2, 6)),
            dma((2, 6)),
            dma((2, 6)),
            dma((2, 2)),
            dma((2, 12)),
            dma((2, 3)),
            dma((2, 3)),
            dma((2, 16)),
        ],
        compiler_params=pltpu.CompilerParams(
            collective_id=0, has_side_effects=True, vmem_limit_bytes=62 * 1024 * 1024
        ),
        name="sublayer",
    )(
        residual_in,
        query_rows.reshape(4, 2, rows // 8, width_in),
        key_rows,
        value_rows,
        out_weight,
        gate_table,
        stretch_order,
        noise_levels,
    )


def solution(mesh):
    placed = (
        P(("ctx", "tp"), None),
        P("ctx", "tp"),
        P("ctx", "tp"),
        P("ctx", "tp"),
        P("tp", None),
        P(),
        P(),
        P(),
    )
    return jax.shard_map(
        on_device, mesh=mesh, in_specs=placed, out_specs=P(("ctx", "tp"), None), check_vma=False
    )
```

time: 98.7 us -> 82.1 us (0.83)
  the two profiles are of different devices: /device:TPU:66 before, /device:TPU:6 now
where the time goes in v2:
time: 82.1 us; the launch traced here: 82 us
  Pallas kernels  80.4 us (98%)
  local copies, waits for them, and re-layouts  1.62 us (2%)
    pallas_call x1, Pallas kernels, on_device(): pl.pallas_call(kernel, out_shape=jax.ShapeDtypeStruct(residual_in.shape,...  80.4 us

profile of v2, /device:TPU:6, one launch (start us, length us, event | category | flops | bytes accessed | tf_op | source)
XLA Modules:
  0.0 82.0 jit_solution(740302704236043581)
XLA Ops:
  0.0 80.4 %sublayer.1 = bf16[16,6144]{1,0:T(8,128)(2,1)} custom-call(bf16[16,6144]{1,0:T(8,128)(2,1)} %res_in.1, bf16[4,2,32,256]{3,2,1,0:T(8,128)(2,1)} %bitcast.1, bf16[256,256]{1,0:T(8,128)(2,1)} %k_in.1, bf16[256,256]{1,0:T(8,128)(2,1)} %v_in.1, bf16[256,6144]{1,0:T(8,128)(2,1)} %w_in.1, bf16[64,6144]{1,0:T(8,128)(2,1)} %gate_in.1, s32[4]{0:T(128)} %order_ref.1, ...), custom_call_target="tpu_custom_call" | custom-call | tf_op jit(solution)/shard_map/sublayer/pallas_call | solution.py:455
  80.4 1.6 %copy.10 = bf16[16,6144]{1,0:T(8,128)(2,1)} copy(bf16[16,6144]{1,0:T(8,128)(2,1)} %sublayer.1) | data formatting | bytes 393216

commit v3 on v2

--- a/solution.py
+++ b/solution.py
@@ -11,6 +11,7 @@
 MESH = pl.DeviceIdType.MESH
 DH = 128
 NEG = -1e30
+BLOCKS = ((0, 1), (1, 2), (2, 4))
 SCALE = math.log2(math.e) / math.sqrt(DH)
 F32 = jnp.float32
 BF16 = jnp.bfloat16
@@ -199,9 +200,7 @@
     for dy in (1, 2, 3):
         send(w_send(dy))
 
-    batch = 4 * rows
-
-    def attend(role, spot):
+    def attend(role, spot, batch):
 
         def load(ref):
             return ref[spot].reshape(batch, DH)
@@ -230,7 +229,7 @@
 
     def attend_part(role, part):
         spot = (slice(None), part)
-        m, total, summed = attend(role, spot)
+        m, total, summed = attend(role, spot, 4 * rows)
         for ref, value in ((peak, m), (lsum, total), (acc, summed)):
             ref[spot] = value.reshape(ref[spot].shape)
 
@@ -285,12 +284,16 @@
     got(k_share[3])
     got(v_share[3])
 
+    def block_rows(j):
+        first, past = BLOCKS[j]
+        return pl.ds(first * rows // 4, (past - first) * rows // 4)
+
     @functools.cache
     def o_back(j, dx):
         index = j * 3 + dx - 1
         return remote(
-            osend.at[j, dx],
-            oret.at[j, dx - 1],
+            osend.at[dx, :, block_rows(j)],
+            oret.at[dx - 1, :, block_rows(j)],
             (ox_sem.at[0, index], ox_sem.at[1, index]),
             xpeer(4 - dx),
         )
@@ -305,15 +308,27 @@
             xpeer(4 - dx),
         )
 
-    for j in (0, 1):
-        m, total, summed = attend(3, (slice(None), slice(None), slice(None), j))
+    for j, (y_first, y_past) in enumerate(BLOCKS):
+        count = y_past - y_first
+        size = count * rows // 4
+        m, total, summed = attend(
+            3, (slice(None), slice(None), slice(None), slice(y_first, y_past)), 8 * size
+        )
         total = jnp.sum(total, axis=1, keepdims=True)
-        osend[j] = (summed * (1.0 / total)).astype(BF16).reshape(4, 2, half, DH)
-        lse = m + jnp.log2(total)
+        result = (summed * (1.0 / total)).astype(BF16).reshape(4, 2, 4, count, rows // 16, DH)
+        lse = (m + jnp.log2(total)).reshape(8, size, DH)
         for dx in range(4):
             for part in (0, 1):
-                first = (2 * dx + part) * half
-                lsend[j, dx, part : part + 1] = lse[first : first + half].T[:1]
+                for step in range(count):
+                    there = pl.ds((y_first + step) * rows // 4, rows // 4)
+                    osend[dx, part, there] = result[dx, part, :, step].reshape(rows // 4, DH)
+                ordered = (
+                    lse[2 * dx + part]
+                    .reshape(4, count, rows // 16, DH)
+                    .swapaxes(0, 1)
+                    .reshape(size, DH)
+                )
+                lsend[j, dx, part : part + 1, :size] = ordered.T[:1]
         for dx in (1, 2, 3):
             send(l_back(j, dx))
             send(o_back(j, dx))
@@ -326,47 +341,52 @@
     seen = [order_ref[(x + dx) % 4] <= place for dx in (1, 2, 3)]
 
     def merged(j, part):
-        states = [(lsend[j, 0, part : part + 1], osend[j, 0, part])]
+        at = block_rows(j)
+        size = at.size
+        states = [(lsend[j, 0, part : part + 1, :size], osend[0, part, at])]
         for dx in (1, 2, 3):
-            lse = jnp.where(seen[dx - 1], lret[j, dx - 1, part : part + 1], NEG)
-            states.append((lse, oret[j, dx - 1, part]))
+            lse = jnp.where(seen[dx - 1], lret[j, dx - 1, part : part + 1, :size], NEG)
+            states.append((lse, oret[dx - 1, part, at]))
         highest = states[0][0]
         for lse, _ in states[1:]:
             highest = jnp.maximum(highest, lse)
         shares = [jnp.exp2(lse - highest) for lse, _ in states]
         total = shares[0] + shares[1] + shares[2] + shares[3]
-        result = jnp.zeros((half, DH), F32)
+        result = jnp.zeros((size, DH), F32)
         for weight, (_, value) in zip(shares, states):
-            result = result + jnp.broadcast_to(weight / total, (DH, DH)).T * value.astype(F32)
+            result = result + jnp.broadcast_to(weight / total, (DH, size)).T * value.astype(F32)
         return result.astype(BF16)
 
+    @functools.cache
     def back(j):
-        return remote(zsend.at[j], abuf.at[j, :, mine], (z_sem.at[0, j], z_sem.at[1, j]), crs)
+        at = block_rows(j)
+        return remote(zsend.at[at], abuf.at[at, mine], (z_sem.at[0, j], z_sem.at[1, j]), crs)
 
     @functools.cache
     def a_send(j, which, dy):
         index = (2 * j + which) * 3 + dy - 1
         lane = head if which == 0 else 1 - head
+        at = block_rows(j)
         there = pl.ds(pl.multiple_of(dy * 2 * DH + lane * DH, DH), DH)
         return remote(
-            abuf.at[j, :, mine if which == 0 else other],
-            abuf.at[j, :, there],
+            abuf.at[at, mine if which == 0 else other],
+            abuf.at[at, there],
             (a_sem.at[0, index], a_sem.at[1, index]),
             ypeer(dy),
         )
 
-    backs = [back(0), back(1)]
-    for j in (0, 1):
+    every = range(len(BLOCKS))
+    for j in every:
         for dx in (1, 2, 3):
             got(l_back(j, dx))
             got(o_back(j, dx))
-        zsend[j] = merged(j, 1)
-        send(backs[j])
-        abuf[j, :, mine] = merged(j, 0)
+        zsend[block_rows(j)] = merged(j, 1)
+        send(back(j))
+        abuf[block_rows(j), mine] = merged(j, 0)
         for dy in (1, 2, 3):
             send(a_send(j, 0, dy))
-    for j in (0, 1):
-        got(backs[j])
+    for j in every:
+        got(back(j))
         for dy in (1, 2, 3):
             send(a_send(j, 1, dy))
 
@@ -379,30 +399,30 @@
 
     def r_send(step):
         there = tpeer(step // 4, step % 4)
-        to_y = there[1] % 4
-        first = pl.ds(pl.multiple_of((there[1] // 4) * 32 + (to_y % 2) * 16, 16), 16)
+        first = pl.ds(pl.multiple_of((there[1] % 4) * 64 + (there[1] // 4) * 16, 16), 16)
         return remote(
-            pbuf.at[to_y // 2, first],
-            rbuf.at[step],
-            (r_sem.at[0, step], r_sem.at[1, step]),
-            there,
-        )
-
-    for j in (0, 1):
+            pbuf.at[first], rbuf.at[step], (r_sem.at[0, step], r_sem.at[1, step]), there
+        )
+
+    for j, (y_first, y_past) in enumerate(BLOCKS):
         for dy in (1, 2, 3):
             got(a_send(j, 0, dy))
             got(a_send(j, 1, dy))
 
         def project(i, carry):
             at = pl.ds(pl.multiple_of(i * piece_width, piece_width), piece_width)
-            pbuf[j, :, at] = jnp.dot(abuf[j], wbuf[:, at], preferred_element_type=F32).astype(BF16)
+            pbuf[block_rows(j), at] = jnp.dot(
+                abuf[block_rows(j)], wbuf[:, at], preferred_element_type=F32
+            ).astype(BF16)
             return carry
 
         lax.fori_loop(0, slab // piece_width, project, 0)
 
+        count = y_past - y_first
+
         def r_start(i, carry):
-            dz = (i // 2 + 1) % 4
-            step = dz * 4 + (2 * j + i % 2 + 4 - y) % 4
+            dz = (i // count + 1) % 4
+            step = dz * 4 + (y_first + i % count + 4 - y) % 4
 
             @pl.when(step != 0)
             def _():
@@ -410,10 +430,10 @@
 
             return carry
 
-        lax.fori_loop(0, 8, r_start, 0)
-
-    own_rows = pl.ds(pl.multiple_of(zl * 32 + (y % 2) * 16, 16), 16)
-    rbuf[0] = pbuf[y // 2, own_rows]
+        lax.fori_loop(0, 4 * count, r_start, 0)
+
+    own_rows = pl.ds(pl.multiple_of(y * 64 + zl * 16, 16), 16)
+    rbuf[0] = pbuf[own_rows]
 
     here(5)
     for dy in (3, 2, 1, 0):
@@ -454,24 +474,24 @@
     dma = pltpu.SemaphoreType.DMA
     return pl.pallas_call(
         kernel,
-        out_shape=jax.ShapeDtypeStruct(residual_in.shape, BF16),
+        out_shape=pltpu.VMEM(residual_in.shape, BF16),
         in_specs=[any_spec] * 6 + [smem_spec] * 2,
         out_specs=pl.BlockSpec(memory_space=pltpu.VMEM),
         scratch_shapes=[
-            pltpu.VMEM((4, 2, 4, 2, rows // 8, DH), BF16),
+            pltpu.VMEM((4, 2, 4, 4, rows // 16, DH), BF16),
             pltpu.VMEM((4, 2, rows, DH), BF16),
             pltpu.VMEM((4, 2, rows, DH), BF16),
-            pltpu.VMEM((4, 2, 4, 2, rows // 8, DH), F32),
-            pltpu.VMEM((4, 2, 4, 2, rows // 8, DH), F32),
-            pltpu.VMEM((4, 2, 4, 2, rows // 8, DH), F32),
-            pltpu.VMEM((2, 4, 2, rows // 2, DH), BF16),
-            pltpu.VMEM((2, 4, 8, DH), F32),
-            pltpu.VMEM((2, 3, 2, rows // 2, DH), BF16),
-            pltpu.VMEM((2, 3, 8, DH), F32),
-            pltpu.VMEM((2, rows // 2, DH), BF16),
-            pltpu.VMEM((2, rows // 2, 8 * DH), BF16),
+            pltpu.VMEM((4, 2, 4, 4, rows // 16, DH), F32),
+            pltpu.VMEM((4, 2, 4, 4, rows // 16, DH), F32),
+            pltpu.VMEM((4, 2, 4, 4, rows // 16, DH), F32),
+            pltpu.VMEM((4, 2, rows, DH), BF16),
+            pltpu.VMEM((len(BLOCKS), 4, 8, DH), F32),
+            pltpu.VMEM((3, 2, rows, DH), BF16),
+            pltpu.VMEM((len(BLOCKS), 3, 8, DH), F32),
+            pltpu.VMEM((rows, DH), BF16),
+            pltpu.VMEM((rows, 8 * DH), BF16),
             pltpu.VMEM((4 * rows, slab), BF16),
-            pltpu.VMEM((2, rows // 2, slab), BF16),
+            pltpu.VMEM((rows, slab), BF16),
             pltpu.VMEM((16, 16, slab), BF16),
             pltpu.VMEM(gate_table.shape, BF16),
             pltpu.VMEM((16, width), F32),
@@ -481,10 +501,10 @@
             dma((2, 4)),
             dma((2, 3)),
             dma((2, 6)),
-            dma((2, 6)),
-            dma((2, 6)),
-            dma((2, 2)),
-            dma((2, 12)),
+            dma((2, 3 * len(BLOCKS))),
+            dma((2, 3 * len(BLOCKS))),
+            dma((2, len(BLOCKS))),
+            dma((2, 6 * len(BLOCKS))),
             dma((2, 3)),
             dma((2, 3)),
             dma((2, 16)),
@@ -495,7 +515,7 @@
         name="sublayer",
     )(
         residual_in,
-        query_rows.reshape(4, 2, rows // 8, width_in),
+        query_rows.reshape(4, 4, rows // 16, width_in),
         key_rows,
         value_rows,
         out_weight,

time: 82.1 us -> 80.3 us (0.978)
  the two profiles are of different devices: /device:TPU:6 before, /device:TPU:2 now
where the time goes in v3:
time: 80.3 us; the launch traced here: 80.2 us
  Pallas kernels  79.5 us (99%)
    pallas_call x1, Pallas kernels, on_device(): pl.pallas_call(kernel, out_shape=pltpu.VMEM(residual_in.shape, BF16), in_...  79.5 us

profile of v3, /device:TPU:2, one launch (start us, length us, event | category | flops | bytes accessed | tf_op | source)
XLA Modules:
  0.0 80.2 jit_solution(17829794640077042192)
XLA Ops:
  0.0 79.5 %sublayer.1 = bf16[16,6144]{1,0:T(8,128)(2,1)S(1)} custom-call(bf16[16,6144]{1,0:T(8,128)(2,1)} %res_in.1, bf16[4,4,16,256]{3,2,1,0:T(8,128)(2,1)} %bitcast.1, bf16[256,256]{1,0:T(8,128)(2,1)} %k_in.1, bf16[256,256]{1,0:T(8,128)(2,1)} %v_in.1, bf16[256,6144]{1,0:T(8,128)(2,1)} %w_in.1, bf16[64,6144]{1,0:T(8,128)(2,1)} %gate_in.1, s32[4]{0:T(128)} %order_ref.1, ...), custom_call_target="tpu_custom_call" | custom-call | tf_op jit(solution)/shard_map/sublayer/pallas_call | solution.py:475
  79.5 0.7 copy.10

commit v4 on v3

--- a/solution.py
+++ b/solution.py
@@ -12,6 +12,7 @@
 DH = 128
 NEG = -1e30
 BLOCKS = ((0, 1), (1, 2), (2, 4))
+PAIRED = (0,)
 SCALE = math.log2(math.e) / math.sqrt(DH)
 F32 = jnp.float32
 BF16 = jnp.bfloat16
@@ -53,6 +54,7 @@
     wbuf,
     pbuf,
     rbuf,
+    sbuf,
     gbuf,
     gsel,
     resbuf,
@@ -68,6 +70,7 @@
     w_sem,
     wf_sem,
     r_sem,
+    s_sem,
 ):
     ctx = lax.axis_index("ctx")
     tp = lax.axis_index("tp")
@@ -404,6 +407,24 @@
             pbuf.at[first], rbuf.at[step], (r_sem.at[0, step], r_sem.at[1, step]), there
         )
 
+    outer = zl % 3 == 0
+    buddy = (ctx, (zl + 1 - 2 * (zl % 2)) * 4 + y)
+
+    def paired(to_y):
+        result = to_y == PAIRED[0]
+        for value in PAIRED[1:]:
+            result = jnp.logical_or(result, to_y == value)
+        return result
+
+    def across(other_zl):
+        return other_zl // 2 != zl // 2
+
+    def pair_rows(n):
+        return pl.ds(pl.multiple_of(PAIRED[n] * 64 + 32 * (1 - zl // 2), 32), 32)
+
+    def pair_send(n):
+        return remote(pbuf.at[pair_rows(n)], sbuf.at[n], (s_sem.at[0, n], s_sem.at[1, n]), buddy)
+
     for j, (y_first, y_past) in enumerate(BLOCKS):
         for dy in (1, 2, 3):
             got(a_send(j, 0, dy))
@@ -418,13 +439,19 @@
 
         lax.fori_loop(0, slab // piece_width, project, 0)
 
+        for n, to_y in enumerate(PAIRED):
+            if y_first <= to_y < y_past:
+                pl.when(outer)(pair_send(n).start)
+
         count = y_past - y_first
 
         def r_start(i, carry):
             dz = (i // count + 1) % 4
-            step = dz * 4 + (y_first + i % count + 4 - y) % 4
-
-            @pl.when(step != 0)
+            to_y = y_first + i % count
+            step = dz * 4 + (to_y + 4 - y) % 4
+            later = jnp.logical_and(paired(to_y), across((zl + dz) % 4))
+
+            @pl.when(jnp.logical_and(step != 0, jnp.logical_not(later)))
             def _():
                 r_send(step).start()
 
@@ -432,28 +459,53 @@
 
         lax.fori_loop(0, 4 * count, r_start, 0)
 
+    for n, to_y in enumerate(PAIRED):
+
+        @pl.when(jnp.logical_not(outer))
+        def _():
+            pair_send(n).wait_recv()
+            at = pair_rows(n)
+            pbuf[at] = (pbuf[at].astype(F32) + sbuf[n].astype(F32)).astype(BF16)
+            for which in (0, 1):
+                to_zl = 2 * (1 - zl // 2) + which
+                r_send((to_zl + 4 - zl) % 4 * 4 + (to_y + 4 - y) % 4).start()
+
     own_rows = pl.ds(pl.multiple_of(y * 64 + zl * 16, 16), 16)
     rbuf[0] = pbuf[own_rows]
 
     here(5)
+    absent = []
+    for dz in range(4):
+        from_zl = (zl + 4 - dz) % 4
+        absent.append(
+            jnp.logical_and(paired(y), jnp.logical_and(across(from_zl), from_zl % 3 == 0))
+        )
     for dy in (3, 2, 1, 0):
         at = columns((y + 4 - dy) % 4)
         for dz in range(4):
             if dz + dy > 0:
-                r_send(4 * dz + dy).wait_recv()
+                pl.when(jnp.logical_not(absent[dz]))(r_send(4 * dz + dy).wait_recv)
         projected = rbuf[dy].astype(F32)
         for dz in (1, 2, 3):
-            projected = projected + rbuf[4 * dz + dy].astype(F32)
+            part = rbuf[4 * dz + dy].astype(F32)
+            projected = projected + jnp.where(absent[dz], 0.0, part)
         mixed = resbuf[:, at].astype(F32) + gsel[:, at] * projected
         out_ref[:, at] = mixed.astype(BF16)
 
     finish()
 
     def r_left(step, carry):
-        r_send(step).wait_send()
+        held = jnp.logical_and(paired((y + step) % 4), across((zl + step // 4) % 4))
+
+        @pl.when(jnp.logical_not(jnp.logical_and(held, outer)))
+        def _():
+            r_send(step).wait_send()
+
         return carry
 
     lax.fori_loop(1, 16, r_left, 0)
+    for n in range(len(PAIRED)):
+        pl.when(outer)(pair_send(n).wait_send)
 
 
 def on_device(
@@ -493,6 +545,7 @@
             pltpu.VMEM((4 * rows, slab), BF16),
             pltpu.VMEM((rows, slab), BF16),
             pltpu.VMEM((16, 16, slab), BF16),
+            pltpu.VMEM((len(PAIRED), 32, slab), BF16),
             pltpu.VMEM(gate_table.shape, BF16),
             pltpu.VMEM((16, width), F32),
             pltpu.VMEM(residual_in.shape, BF16),
@@ -508,6 +561,7 @@
             dma((2, 3)),
             dma((2, 3)),
             dma((2, 16)),
+            dma((2, len(PAIRED))),
         ],
         compiler_params=pltpu.CompilerParams(
             collective_id=0, has_side_effects=True, vmem_limit_bytes=62 * 1024 * 1024

time: 80.3 us -> 78.2 us (0.974)
  the two profiles are of different devices: /device:TPU:2 before, /device:TPU:6 now
where the time goes in v4:
time: 78.2 us; the launch traced here: 76.8 us
  Pallas kernels  76.1 us (97%)
    pallas_call x1, Pallas kernels, on_device(): pl.pallas_call(kernel, out_shape=pltpu.VMEM(residual_in.shape, BF16), in_...  76.1 us

profile of v4, /device:TPU:6, one launch (start us, length us, event | category | flops | bytes accessed | tf_op | source)
XLA Modules:
  0.0 76.8 jit_solution(16011421458887291533)
XLA Ops:
  0.0 76.1 %sublayer.1 = bf16[16,6144]{1,0:T(8,128)(2,1)S(1)} custom-call(bf16[16,6144]{1,0:T(8,128)(2,1)} %res_in.1, bf16[4,4,16,256]{3,2,1,0:T(8,128)(2,1)} %bitcast.1, bf16[256,256]{1,0:T(8,128)(2,1)} %k_in.1, bf16[256,256]{1,0:T(8,128)(2,1)} %v_in.1, bf16[256,6144]{1,0:T(8,128)(2,1)} %w_in.1, bf16[64,6144]{1,0:T(8,128)(2,1)} %gate_in.1, s32[4]{0:T(128)} %order_ref.1, ...), custom_call_target="tpu_custom_call" | custom-call | tf_op jit(solution)/shard_map/sublayer/pallas_call | solution.py:527
  76.2 0.7 copy.10

commit v5 on v4

--- a/solution.py
+++ b/solution.py
@@ -11,7 +11,7 @@
 MESH = pl.DeviceIdType.MESH
 DH = 128
 NEG = -1e30
-BLOCKS = ((0, 1), (1, 2), (2, 4))
+BLOCKS = ((0, 1), (1, 3), (3, 4))
 PAIRED = (0,)
 SCALE = math.log2(math.e) / math.sqrt(DH)
 F32 = jnp.float32

time: 78.2 us -> 77.5 us (level)
  no operation moved by 1% of the time
where the time goes in v5:
time: 77.5 us; the launch traced here: 76.6 us
  Pallas kernels  75.9 us (98%)
    pallas_call x1, Pallas kernels, on_device(): pl.pallas_call(kernel, out_shape=pltpu.VMEM(residual_in.shape, BF16), in_...  75.9 us

profile of v5, /device:TPU:6, one launch (start us, length us, event | category | flops | bytes accessed | tf_op | source)
XLA Modules:
  0.0 76.6 jit_solution(6055920165719303570)
XLA Ops:
  0.0 75.9 %sublayer.1 = bf16[16,6144]{1,0:T(8,128)(2,1)S(1)} custom-call(bf16[16,6144]{1,0:T(8,128)(2,1)} %res_in.1, bf16[4,4,16,256]{3,2,1,0:T(8,128)(2,1)} %bitcast.1, bf16[256,256]{1,0:T(8,128)(2,1)} %k_in.1, bf16[256,256]{1,0:T(8,128)(2,1)} %v_in.1, bf16[256,6144]{1,0:T(8,128)(2,1)} %w_in.1, bf16[64,6144]{1,0:T(8,128)(2,1)} %gate_in.1, s32[4]{0:T(128)} %order_ref.1, ...), custom_call_target="tpu_custom_call" | custom-call | tf_op jit(solution)/shard_map/sublayer/pallas_call | solution.py:527
  75.9 0.7 copy.10

commit v6 on v5

--- a/solution.py
+++ b/solution.py
@@ -446,7 +446,8 @@
         count = y_past - y_first
 
         def r_start(i, carry):
-            dz = (i // count + 1) % 4
+            turn = i // count
+            dz = (turn + 2) * (1 - turn // 2) + (3 - turn) * (turn // 2)
             to_y = y_first + i % count
             step = dz * 4 + (to_y + 4 - y) % 4
             later = jnp.logical_and(paired(to_y), across((zl + dz) % 4))

time: 77.5 us -> 77.9 us (level)
  the two profiles are of different devices: /device:TPU:6 before, /device:TPU:24 now
where the time goes in v6:
time: 77.9 us; the launch traced here: 77.7 us
  Pallas kernels  77.1 us (99%)
    pallas_call x1, Pallas kernels, on_device(): pl.pallas_call(kernel, out_shape=pltpu.VMEM(residual_in.shape, BF16), in_...  77.1 us

profile of v6, /device:TPU:24, one launch (start us, length us, event | category | flops | bytes accessed | tf_op | source)
XLA Modules:
  0.0 77.7 jit_solution(1413667439104585852)
XLA Ops:
  0.0 77.1 %sublayer.1 = bf16[16,6144]{1,0:T(8,128)(2,1)S(1)} custom-call(bf16[16,6144]{1,0:T(8,128)(2,1)} %res_in.1, bf16[4,4,16,256]{3,2,1,0:T(8,128)(2,1)} %bitcast.1, bf16[256,256]{1,0:T(8,128)(2,1)} %k_in.1, bf16[256,256]{1,0:T(8,128)(2,1)} %v_in.1, bf16[256,6144]{1,0:T(8,128)(2,1)} %w_in.1, bf16[64,6144]{1,0:T(8,128)(2,1)} %gate_in.1, s32[4]{0:T(128)} %order_ref.1, ...), custom_call_target="tpu_custom_call" | custom-call | tf_op jit(solution)/shard_map/sublayer/pallas_call | solution.py:528
  77.1 0.7 copy.10
